TPU v7x, 32 devices: a whole 2x2x4 slice. The times are simulated.
32 devices in a mesh: groups: 2 (over y), row: 4 (over x, core), col: 4 (over z).
Axes of the slice: x: 2, y: 2, z: 4, core: 2. Of those that a mesh axis runs over, the one named last changes fastest.
Arguments:
- tile_bits: int32 [8, 4, 96, 32, 256], P(('groups', 'row'), 'col'), parts along dimension 0, may hold values from 0 to 255
- tile_rows: int32 [8, 4, 96], P(('groups', 'row'), 'col'), parts along dimension 0, may hold values from 0 to 3
- tile_cols: int32 [8, 4, 96], P(('groups', 'row'), 'col'), parts along dimension 0, may hold values from 0 to 3
- tile_count: int32 [8, 4], P(('groups', 'row'), 'col'), parts along dimension 0, may hold values from 12 to 96, as said below
- host_order: int32 [8192], P('groups'), parts along dimension 0, may hold values from 0 to 4095, each once
- seed_hosts: int32 [256, 256], P('groups'), parts along dimension 0, may hold values from 0 to 4095
- dangling: int32 [8192], P(('groups', 'col')), parts along dimension 0, may hold values 0 or 1
Outputs:
- rank: float32 [8192, 128], P(('groups', 'row', 'col')), parts along dimension 0
- change: float32 [256], P('groups'), parts along dimension 0
There are 2 independent parts, one for each index of `groups`. A program takes and returns all parts, laid end to end along the dimension named above; each array names one. Nothing has to cross between parts.
Inputs may be any that keep to these rules, and one draw needn't show every extreme that they name: `tile_count`: slots at or past a cell's count hold data that is not part of the graph. Some cell has exactly 96 live slots. `tile_rows`: slots of one cell may name the same block pair; their tiles add.
All inputs are finite; a program needn't handle non-finite values. No bound on the sum of `dangling` on one device may be relied on, other than what follows from the above.
Results may differ from a plain program's by a relative error of at most 0.002.
Values may be sent and summed in bfloat16 or wider, within the bound.
A program may use at most 64 MiB of HBM per device.

v0:
```python
import jax
import jax.numpy as jnp
from jax import lax
from jax.sharding import PartitionSpec as P

ITERS = 2


slot_group = 8


def from_root(block, axis, holder):
    block = jnp.where(lax.axis_index(axis) == holder, block, jnp.zeros_like(block))
    return lax.psum(block, axis)


def unpack(packed_words):
    bit_shift = jnp.arange(8, dtype=jnp.int32)
    bit_values = jnp.right_shift(packed_words[..., :, None, :], bit_shift[:, None]) & 1
    shape = packed_words.shape
    return bit_values.reshape(shape[:-2] + (shape[-2] * 8, shape[-1]))


def teleport_rows(positions, first_host, row_count, seed_scale):
    local_rows = positions - first_host
    inside = (local_rows >= 0) & (local_rows < row_count)
    target_rows = jnp.where(inside, local_rows, row_count)
    topic_ids = jnp.broadcast_to(
        jnp.arange(positions.shape[0], dtype=jnp.int32)[:, None], positions.shape
    )
    empty = jnp.zeros((row_count, positions.shape[0]), jnp.float32)
    return empty.at[target_rows, topic_ids].add(seed_scale, mode="drop")


def shards(tile_bits, tile_rows, tile_cols, tile_count, host_order, seed_hosts, dangling):
    packed = tile_bits[0, 0]
    slot_rows = tile_rows[0, 0]
    slot_cols = tile_cols[0, 0]
    live_count = tile_count[0, 0]
    host_total = host_order.shape[0]
    range_hosts = dangling.shape[0]
    block_size = packed.shape[2]
    range_blocks = range_hosts // block_size
    topics = seed_hosts.shape[0]
    piece_rows = range_hosts // lax.axis_size("col")
    row_index = lax.axis_index("row")
    col_index = lax.axis_index("col")
    seed_scale = host_total / (16.0 * seed_hosts.shape[1])
    positions = host_order[seed_hosts]
    block_ids = jnp.arange(range_blocks, dtype=jnp.int32)
    group_count = (live_count + slot_group - 1) // slot_group

    def group_tiles(group):
        first_slot = group * slot_group
        packed_words = lax.dynamic_slice_in_dim(packed, first_slot, slot_group, 0)
        live_slots = first_slot + jnp.arange(slot_group, dtype=jnp.int32) < live_count
        dense_tiles = (unpack(packed_words) * live_slots.astype(jnp.int32)[:, None, None]).astype(
            jnp.bfloat16
        )
        group_rows = lax.dynamic_slice_in_dim(slot_rows, first_slot, slot_group, 0)
        group_cols = lax.dynamic_slice_in_dim(slot_cols, first_slot, slot_group, 0)
        return (dense_tiles, group_rows, group_cols)

    def add_degree(group, running):
        dense_tiles, group_rows, group_cols = group_tiles(group)
        col_sums = jnp.sum(dense_tiles.astype(jnp.float32), axis=1)
        placing = (group_cols[:, None] == block_ids[None, :]).astype(jnp.float32)
        return running + jnp.einsum("gb,gj->bj", placing, col_sums, precision=lax.Precision.HIGHEST)

    local_degree = lax.fori_loop(
        0, group_count, add_degree, jnp.zeros((range_blocks, block_size), jnp.float32)
    )
    degree = lax.psum(local_degree, "row").reshape(range_hosts)
    weight = (1.0 - dangling.astype(jnp.float32)) / jnp.maximum(degree, 1.0)

    def own_flow(flow_full):
        return lax.psum_scatter(flow_full, "col", scatter_dimension=0, tiled=True)

    def lost_total(rank_own, flow_own):
        return lax.psum(jnp.sum(rank_own, axis=0) - jnp.sum(flow_own, axis=0), ("row", "col"))

    def advance(flow, teleport, lost_share):
        return 0.85 * flow + (0.85 * lost_share / (host_total / 16.0) + 0.15) * teleport

    first_own = row_index * range_hosts + col_index * piece_rows
    tele_own = teleport_rows(positions, first_own, piece_rows, seed_scale)
    rank_own = tele_own
    source_bf = teleport_rows(positions, col_index * range_hosts, range_hosts, seed_scale).astype(
        jnp.bfloat16
    )
    change = jnp.zeros((topics,), jnp.float32)
    for iteration in range(ITERS):
        scaled = (source_bf.astype(jnp.float32) * weight[:, None]).astype(jnp.bfloat16)
        scaled_blocks = scaled.reshape(range_blocks, block_size, topics)

        def add_group(group, running):
            dense_tiles, group_rows, group_cols = group_tiles(group)
            picking = (group_cols[:, None] == block_ids[None, :]).astype(jnp.bfloat16)
            sources = jnp.einsum(
                "gb,bjk->gjk", picking, scaled_blocks, preferred_element_type=jnp.float32
            ).astype(jnp.bfloat16)
            product = jnp.einsum(
                "gij,gjk->gik", dense_tiles, sources, preferred_element_type=jnp.float32
            )
            placing = (group_rows[:, None] == block_ids[None, :]).astype(jnp.float32)
            return running + jnp.einsum(
                "gb,gik->bik", placing, product, precision=lax.Precision.HIGHEST
            )

        start = jnp.zeros((range_blocks, block_size, topics), jnp.float32)
        flow_full = lax.fori_loop(0, group_count, add_group, start).reshape(range_hosts, topics)
        if iteration + 1 < ITERS:
            flow_own = own_flow(flow_full)
            lost_share = lost_total(rank_own, flow_own)
            rank_own = advance(flow_own, tele_own, lost_share)
            range_ranks = lax.all_gather(rank_own.astype(jnp.bfloat16), "col", axis=0, tiled=True)
            source_bf = from_root(range_ranks, "row", col_index)
        else:
            flow_own = own_flow(flow_full)
            lost_share = lost_total(rank_own, flow_own)
            new_rank = advance(flow_own, tele_own, lost_share)
            change = (
                lax.psum(jnp.sum(jnp.abs(new_rank - rank_own), axis=0), ("row", "col")) / host_total
            )
            rank_own = new_rank
    return (rank_own, change)


def solution(mesh):
    in_specs = (
        P(("groups", "row"), "col", None, None, None),
        P(("groups", "row"), "col", None),
        P(("groups", "row"), "col", None),
        P(("groups", "row"), "col"),
        P("groups"),
        P("groups", None),
        P(("groups", "col")),
    )
    out_specs = (P(("groups", "row", "col"), None), P("groups"))
    return jax.shard_map(shards, mesh=mesh, in_specs=in_specs, out_specs=out_specs, check_vma=False)
```

profile of v0, /device:TPU:0, one launch (start us, length us, event | category | flops | bytes accessed | tf_op | source)
XLA Modules:
  0.0 845.6 jit_solution(13563468083352317062)
XLA Ops:
  8.9 180.5 %gather_fusion = s32[32768]{0:T(1024)S(1)} fusion(s32[4096]{0:T(1024)S(1)} %copy-done, s32[32768]{0:T(1024)S(1)} %broadcast_clamp_fusion), kind=kCustom, calls=%fused_computation | custom fusion | bytes 393216 | tf_op jit(solution)/shard_map/gather | solution.py:49
  190.5 28.5 %while.35 = (s32[]{:T(128)}, f32[4,256]{1,0:T(4,128)S(1)}, s32[]{:T(128)}, s32[96]{0:T(128)S(1)}, s32[96,32,256]{2,1,0:T(8,128)}, /*index=5*/s32[]{:T(128)}, s32[]{:T(128)}, s32[]{:T(128)}, s32[]{:T(128)}, s32[]{:T(128)}) while((s32[]{:T(128)}, f32[4,256]{1,0:T(4,128)S(1)}, s32[]{:T(128)}, s32[96]{0:T(128)S(1)}, ...), condition=%wide.region_3.4_spmd.clone, body=%wide.region_1.0_spmd.clone.sunk | while | flops 3243070 | bytes 811339 | solution.py:70
  219.0 8.0 psum.35
  227.1 171.2 %scatter_custom_fusion = f32[131072]{0:T(1024)S(1)} fusion(s32[32768]{0:T(1024)S(1)} %bitcast.91, f32[32768]{0:T(1024)S(1)} %broadcast.239, f32[]{:T(128)} %constant.44.clone.1), kind=kCustom, calls=%fused_computation.65 | custom fusion | flops 32768 | bytes 524292
  398.8 51.2 %while.36 = (s32[]{:T(128)}, f32[4,256,128]{2,0,1:T(4,128)S(1)}, s32[]{:T(128)}, s32[96]{0:T(128)S(1)}, s32[96,32,256]{2,1,0:T(8,128)}, /*index=5*/s32[]{:T(128)...) while((s32[]{:T(128)}, f32[4,256,128]{2,0,1:T(4,128)S(1)}, ...), condition=%wide.region_6.7_spmd.clone.clone, body=%wide.region_5.6_spmd.clone.clone.sunk | while | flops 151388256 | bytes 5247423 | solution.py:111
  401.6 1.4 convolution_add_fusion.7
  405.9 1.4 convolution_add_fusion.7
  410.1 1.4 convolution_add_fusion.7
  414.4 1.4 convolution_add_fusion.7
  418.7 1.4 convolution_add_fusion.7
  422.9 1.4 convolution_add_fusion.7
  427.2 1.4 convolution_add_fusion.7
  451.0 171.1 %scatter_custom_fusion.1 = f32[32768]{0:T(1024)S(1)} fusion(s32[32768]{0:T(1024)S(1)} %bitcast.92, f32[32768]{0:T(1024)S(1)} %broadcast.239, f32[]{:T(128)} %constant.44.clone.1), kind=kCustom, calls=%fused_computation.84 | custom fusion | flops 32768 | bytes 131076
  623.1 30.4 %psum.36 = f32[128]{0:T(128)S(1)} all-reduce(f32[128]{0:T(128)S(1)} %sub.60), channel_id=1, replica_groups=mesh['groups'=2,'row'=4,'col'=4] {'row','col'}, use_global_device_ids=true, to_apply=%region_11.12 | all-reduce | flops 128 | bytes 1024 | tf_op jit(solution)/shard_map/psum | solution.py:80
  654.5 13.9 %all_gather.3 = bf16[1024,128]{1,0:T(8,128)(2,1)S(1)} all-gather(bf16[256,128]{1,0:T(8,128)(2,1)S(1)} %convert_element_type.71), channel_id=1, replica_groups=mesh['groups'=2,'row'=4,'col'=4] {'col'}, dimensions={0}, use_global_device_ids=true | all-gather | bytes 327680 | tf_op jit(solution)/shard_map/all_gather | solution.py:116
  669.1 31.3 %all-reduce.2.cloned.1.call-done = bf16[1024,128]{1,0:T(8,128)(2,1)} async-done(((bf16[1024,128]{1,0:T(8,128)(2,1)}), bf16[1024,128]{1,0:T(8,128)(2,1)}) %all-reduce.2.cloned.1.call-update) | async-done | bytes 262160 | tf_op jit(solution)/shard_map/psum | solution.py:14
  701.9 51.2 %while.37 = (s32[]{:T(128)}, f32[4,256,128]{2,0,1:T(4,128)S(1)}, s32[]{:T(128)}, s32[96]{0:T(128)S(1)}, s32[96,32,256]{2,1,0:T(8,128)}, /*index=5*/s32[]{:T(128)...) while((s32[]{:T(128)}, f32[4,256,128]{2,0,1:T(4,128)S(1)}, ...), condition=%wide.region_14.15_spmd.clone.clone, body=%wide.region_13.14_spmd.clone.clone.sunk | while | flops 151388256 | bytes 5247423 | solution.py:111
  713.3 1.4 convolution_add_fusion.8
  717.5 1.4 convolution_add_fusion.8
  730.3 1.4 convolution_add_fusion.8
  754.0 20.5 %reduce-scatter.5.cloned.1.call-done = f32[256,128]{1,0:T(8,128)} async-done(((f32[1024,128]{1,0:T(8,128)}), f32[256,128]{1,0:T(8,128)}) %reduce-scatter.5.cloned.1.call-update) | async-done | bytes 131088 | tf_op jit(solution)/shard_map/reduce_scatter | solution.py:77
  775.4 29.8 %psum.38 = f32[128]{0:T(128)S(1)} all-reduce(f32[128]{0:T(128)S(1)} %sub.61), channel_id=1, replica_groups=mesh['groups'=2,'row'=4,'col'=4] {'row','col'}, use_global_device_ids=true, to_apply=%region_18.19 | all-reduce | flops 128 | bytes 1024 | tf_op jit(solution)/shard_map/psum | solution.py:80
  805.1 1.6 abs_reduce_fusion
  806.7 31.8 %psum.39 = f32[128]{0:T(128)S(1)} all-reduce(f32[128]{0:T(128)S(1)} %get-tuple-element.308), channel_id=1, replica_groups=mesh['groups'=2,'row'=4,'col'=4] {'row','col'}, use_global_device_ids=true, to_apply=%region_20.21 | all-reduce | flops 128 | bytes 1024 | tf_op jit(solution)/shard_map/psum | solution.py:123
  (325 shorter events, 124.9 us)
Async XLA Ops:
  7.2 1.8 copy-start
  7.2 614.9 %reduce-scatter.3.cloned.1.call-start = ((), (), s32[]{:S(2)}) async-start(), calls=%async_computation.2 | async-start | bytes 655360 | tf_op jit(solution)/shard_map/reduce_scatter | solution.py:77
  8.9 180.8 %copy-start.4 = (s32[2]{0:T(128)S(1)}, s32[2]{0:T(128)}, u32[]{:S(2)}) copy-start(s32[2]{0:T(128)} %constant.96) | copy-start | bytes 28
  189.5 0.7 copy-start.2
  189.5 0.7 copy-start.3
  189.5 1.0 copy-start.6
  190.5 36.6 %copy-start.1 = (s32[1024]{0:T(1024)S(1)}, s32[1024]{0:T(1024)}, u32[]{:S(2)}) copy-start(s32[1024]{0:T(1024)} %param.19) | copy-start | bytes 12292
  219.0 179.8 %copy-start.5 = (s32[1,1,96]{2,1,0:T(1,128)S(1)}, s32[1,1,96]{2,1,0:T(1,128)}, u32[]{:S(2)}) copy-start(s32[1,1,96]{2,1,0:T(1,128)} %param.14) | copy-start | bytes 1156
  450.8 249.6 %all-reduce.2.cloned.1.call-start = ((), (), s32[]{:S(2)}) async-start(), calls=%async_computation.3 | async-start | bytes 524288 | tf_op jit(solution)/shard_map/psum | solution.py:14
  669.1 105.3 %reduce-scatter.5.cloned.1.call-start = ((), (), s32[]{:S(2)}) async-start(), calls=%async_computation.4 | async-start | bytes 655360 | tf_op jit(solution)/shard_map/reduce_scatter | solution.py:77
Sparse Core Ops, SparseCore 0:
  451.0 20.8 reduce-scatter.2
  669.2 31.1 all-reduce.1
  754.1 20.2 reduce-scatter.4
where the time goes:
time: 848 us; the launch traced here: 846 us
  other arithmetic  379 us (45%)
  local copies, waits for them, and re-layouts  225 us (27%)
  blocking collectives  114 us (13%)
  matrix products  59.3 us (7%)
  waiting for transfers between devices  51.8 us (6%)
  between operations  14.7 us (2%)
    unnamed x7, other arithmetic  343 us
    gather x1, local copies, waits for them, and re-layouts, shards(): positions = host_order[seed_hosts]  181 us
    psum x2, blocking collectives, lost_total(): lax.psum(jnp.sum(rank_own, axis=0) - jnp.sum(flow_own, axis=0), ('row', '...  60.2 us
    dynamic_slice x36, local copies, waits for them, and re-layouts, group_tiles(): packed_words = lax.dynamic_slice_in_dim(packed, first_slot, slot_group, 0)  35 us
    dot_general x24, matrix products, add_group(): jnp.einsum('gb,gik->bik', placing, product, precision=lax.Precision.HIGHEST)  34.2 us
    psum x1, blocking collectives, shards(): lax.psum(jnp.sum(jnp.abs(new_rank - rank_own), axis=0), ('row', 'col'))  31.8 us
    psum x1, waiting for transfers between devices, from_root(): return lax.psum(block, axis)  31.3 us
    convert_element_type x36, other arithmetic, group_tiles(): live_slots.astype(jnp.int32)[:, None, None]  23.5 us
  transfers between devices with their start and end apart: 3, of which 2 were waited for; matrix products, arithmetic and copies ran while one was open for 20% of the time, Pallas kernels for 0%

commit v1 on v0

v1 whole, which is shorter than its diff:
```python
import functools

import jax
import jax.numpy as jnp
from jax import lax
from jax.experimental import pallas as pl
from jax.experimental.pallas import tpu as pltpu
from jax.sharding import PartitionSpec as P

LANES = 128
MESH = pl.DeviceIdType.MESH


def cell_kernel(
    sizes, rows_ref, cols_ref, count_ref, bits_hbm, order_ref, seeds_ref,
    a_ref, deg_ref, src_ref, own_ref, bits, acc, dacc, pos, hist, sem,
):
    range_hosts, piece, block, blocks, seed_scale = sizes
    words = block // 8
    topics, seeds = seeds_ref.shape
    row_index = lax.axis_index("row")
    col_index = lax.axis_index("col")
    fetch = pltpu.make_async_copy(bits_hbm, bits, sem)
    fetch.start()
    acc[...] = jnp.zeros_like(acc)
    dacc[...] = jnp.zeros_like(dacc)

    table_rows = order_ref.shape[0]
    parts = seeds // LANES

    def place(group, carry):
        rows8 = pl.ds(pl.multiple_of(group * 8, 8), 8)
        ids = [seeds_ref[rows8, h * LANES:(h + 1) * LANES] for h in range(parts)]
        low = [x & (LANES - 1) for x in ids]
        high = [x >> 7 for x in ids]

        def look(t, found):
            row = jnp.broadcast_to(order_ref[pl.ds(t, 1), :], (8, LANES))
            return tuple(
                jnp.where(high[h] == t,
                          jnp.take_along_axis(row, low[h], axis=1, mode="promise_in_bounds"),
                          found[h])
                for h in range(parts)
            )

        found = lax.fori_loop(0, table_rows, look,
                              tuple(jnp.zeros((8, LANES), jnp.int32) for _ in range(parts)),
                              unroll=8)
        for h in range(parts):
            pos[rows8, h * LANES:(h + 1) * LANES] = found[h]
        return carry

    lax.fori_loop(0, topics // 8, place, 0)

    src_high = range_hosts // LANES
    own_high = piece // LANES
    high_rows = hist.shape[0] // topics
    t = lax.broadcasted_iota(jnp.int32, (high_rows, seeds), 0)
    first_src = col_index * src_high
    first_own = row_index * src_high + col_index * own_high
    wanted = jnp.where(t < src_high, first_src + t,
                       jnp.where(t < src_high + own_high, first_own + t - src_high, -1))
    lane_id = lax.broadcasted_iota(jnp.int32, (LANES, seeds), 0)

    def count(k, carry):
        row = pos[pl.ds(k, 1), :]
        low = jnp.where((row & (LANES - 1)) == lane_id, 1.0, 0.0).astype(jnp.bfloat16)
        high = jnp.where((row >> 7) == wanted, 1.0, 0.0).astype(jnp.bfloat16)
        hist[pl.ds(pl.multiple_of(k * high_rows, 8), high_rows), :] = lax.dot_general(
            high, low, (((1,), (1,)), ((), ())), preferred_element_type=jnp.float32)
        return carry

    lax.fori_loop(0, topics, count, 0, unroll=8)
    for i in range(src_high):
        src_ref[i * LANES:(i + 1) * LANES, :] = (
            hist[pl.ds(i, topics, stride=high_rows), :].T * seed_scale)
    for i in range(own_high):
        own_ref[i * LANES:(i + 1) * LANES, :] = (
            hist[pl.ds(src_high + i, topics, stride=high_rows), :].T * seed_scale)

    fetch.wait()

    def add_tile(s, carry):
        pair = rows_ref[s] * blocks + cols_ref[s]
        w = bits[s]
        w = w | (w << 7)
        w = w | (w << 14)
        acc[pair, 0] = acc[pair, 0] + (w & 0x01010101)
        acc[pair, 1] = acc[pair, 1] + ((w >> 4) & 0x01010101)
        return carry

    lax.fori_loop(0, count_ref[0], add_tile, 0)

    def expand(pair, carry):
        first_row = (pair // blocks) * block
        col = pair % blocks
        cols = pl.ds(pl.multiple_of(col * block, block), block)
        total = dacc[col]
        for half in range(2):
            packed = acc[pair, half]
            for b in range(4):
                v = (packed >> (8 * b)) & 255
                total = total + v
                start = pl.multiple_of(first_row + (half * 4 + b) * words, 16)
                a_ref[pl.ds(start, words), cols] = v.astype(jnp.float32).astype(jnp.bfloat16)
        dacc[col] = total
        return carry

    lax.fori_loop(0, blocks * blocks, expand, 0)
    per = block // LANES
    for col in range(blocks):
        sums = jnp.sum(dacc[col], axis=0, keepdims=True).astype(jnp.float32)
        for i in range(per):
            deg_ref[col * per + i:col * per + i + 1, :] = sums[:, i * LANES:(i + 1) * LANES]


def rank_kernel(
    sizes, a_ref, deg_ref, dang_ref, src_ref, own_ref, rank_ref, change_ref,
    degs, wrow, drow, wcol, dcol, scaled, nat, own_flow, sbuf1, sbuf2, recv_b, recv_c, recv_t,
    rank1, recv_d, lost1, lost2, chg,
    deg_s, deg_r, l1_s, l1_r, l2_s, l2_r, b_s, b_r, c_s, c_r, t_s, t_r, d_s, d_r, e_s, e_r,
):
    n_row, n_col, range_hosts, piece, block, host_total = sizes
    words = block // 8
    r = lax.axis_index("row")
    c = lax.axis_index("col")
    me = r * n_col + c
    total_mass = host_total / 16.0
    chunks = range_hosts // LANES

    def each(n, body):
        lax.fori_loop(0, n, lambda i, carry: (body(i), carry)[1], 0)

    def others(n, mine, body):
        def step(i):
            @pl.when(i != mine)
            def _():
                body(i)
        each(n, step)

    def remote(src, dst, send, recv, row, col):
        return pltpu.make_async_remote_copy(
            src_ref=src, dst_ref=dst, send_sem=send, recv_sem=recv,
            device_id={"row": row, "col": col}, device_id_type=MESH)

    barrier = pltpu.get_barrier_semaphore()
    others(n_row * n_col, me, lambda i: pl.semaphore_signal(
        barrier, inc=1, device_id={"row": i // n_col, "col": i % n_col}, device_id_type=MESH))
    pl.semaphore_wait(barrier, n_row * n_col - 1)

    def deg_copy(i, slot):
        return remote(deg_ref, degs.at[slot], deg_s.at[i], deg_r.at[slot], i, c)

    others(n_row, r, lambda i: deg_copy(i, r).start())
    degs[r] = deg_ref[...]
    others(n_row, r, lambda i: deg_copy(i, i).wait_recv())
    degree = degs[0]
    for i in range(1, n_row):
        degree = degree + degs[i]
    wrow[...] = (1.0 - dang_ref[...].astype(jnp.float32)) / jnp.maximum(degree, 1.0)
    drow[...] = degree

    def spread(i):
        rows = pl.ds(pl.multiple_of(i * LANES, LANES), LANES)
        wcol[rows, :] = jnp.broadcast_to(wrow[pl.ds(i, 1), :], (LANES, LANES)).T
        dcol[rows, :] = jnp.broadcast_to(drow[pl.ds(i, 1), :], (LANES, LANES)).T

    each(chunks, spread)

    def make_scaled(source_of, lost, send, recv):
        def step(i, total):
            rows = pl.ds(pl.multiple_of(i * LANES, LANES), LANES)
            part = (source_of(i, rows).astype(jnp.float32) * wcol[rows, :]).astype(jnp.bfloat16)
            scaled[rows, :] = part
            mass = dcol[rows, :] * part.astype(jnp.float32)
            return total + jnp.sum(mass.reshape(LANES // 8, 8, LANES), axis=0)

        lost[c] = lax.fori_loop(0, chunks, step, jnp.zeros((8, LANES), jnp.float32))
        others(n_col, c, lambda i: lost_copy(lost, send, recv, i, c).start())

    def lost_copy(lost, send, recv, i, slot):
        return remote(lost.at[c], lost.at[slot], send.at[i], recv.at[slot], r, i)

    def coefficient(lost, send, recv):
        others(n_col, c, lambda i: lost_copy(lost, send, recv, i, i).wait_recv())
        total = lost[0]
        for i in range(1, n_col):
            total = total + lost[i]
        gone = total_mass - jnp.sum(total, axis=0, keepdims=True)
        return 0.85 * gone / total_mass + 0.15

    def flow_piece(q, sbuf):
        for sub in range(piece // block):
            first = pl.multiple_of(q * piece + sub * block, block)
            product = jnp.dot(a_ref[pl.ds(first, block), :], scaled[...],
                              preferred_element_type=jnp.float32)
            for bit in range(8):
                nat[pl.ds(sub * block + bit, words, stride=8), :] = (
                    product[bit * words:(bit + 1) * words, :])
        sbuf[q] = nat[...].astype(jnp.bfloat16)

    make_scaled(lambda i, rows: src_ref[rows, :].astype(jnp.bfloat16), lost1, l1_s, l1_r)
    diagonal = r == c

    def b_copy(q, slot):
        return remote(sbuf1.at[q], recv_b.at[slot], b_s.at[q], b_r.at[slot], q, r)

    def first_piece(i):
        q = lax.rem(r + 1 + i, n_row)
        flow_piece(q, sbuf1)
        home = jnp.logical_and(diagonal, q == r)

        @pl.when(jnp.logical_not(home))
        def _():
            b_copy(q, c).start()

        @pl.when(home)
        def _():
            recv_b[c] = sbuf1[q]

    each(n_row, first_piece)
    share1 = coefficient(lost1, l1_s, l1_r)

    def b_wait(i):
        @pl.when(jnp.logical_not(jnp.logical_and(diagonal, i == c)))
        def _():
            b_copy(0, i).wait_recv()

    each(n_col, b_wait)
    flow = recv_b[0].astype(jnp.float32)
    for i in range(1, n_col):
        flow = flow + recv_b[i].astype(jnp.float32)
    tele = src_ref[pl.ds(pl.multiple_of(r * piece, piece), piece), :]
    new_rank = 0.85 * flow + share1 * tele
    recv_c[r] = new_rank.astype(jnp.bfloat16)

    def c_copy(i, slot):
        return remote(recv_c.at[r], recv_c.at[slot], c_s.at[i], c_r.at[slot], i, c)

    others(n_row, r, lambda i: c_copy(i, r).start())
    rank1[...] = new_rank
    t_copy = remote(rank1, recv_t, t_s, t_r, c, r)

    @pl.when(jnp.logical_not(diagonal))
    def _():
        t_copy.start()

    @pl.when(diagonal)
    def _():
        recv_t[...] = rank1[...]

    others(n_row, r, lambda i: c_copy(i, i).wait_recv())

    per = piece // LANES

    def second_source(i, rows):
        inner = pl.ds(pl.multiple_of((i % per) * LANES, LANES), LANES)
        return recv_c[i // per, inner, :]

    make_scaled(second_source, lost2, l2_s, l2_r)

    def d_copy(q, slot):
        return remote(sbuf2.at[q], recv_d.at[slot], d_s.at[q], d_r.at[slot], r, q)

    def second_piece(i):
        q = lax.rem(c + 1 + i, n_col)
        flow_piece(q, sbuf2)

        @pl.when(q != c)
        def _():
            d_copy(q, c).start()

        @pl.when(q == c)
        def _():
            own_flow[...] = nat[...]

    each(n_col, second_piece)
    share2 = coefficient(lost2, l2_s, l2_r)
    recv_d[c] = jnp.zeros((piece, LANES), jnp.bfloat16)

    @pl.when(jnp.logical_not(diagonal))
    def _():
        t_copy.wait_recv()

    others(n_col, c, lambda i: d_copy(0, i).wait_recv())
    flow = own_flow[...]
    for i in range(n_col):
        flow = flow + recv_d[i].astype(jnp.float32)
    last = 0.85 * flow + share2 * own_ref[...]
    moved = jnp.abs(last - recv_t[...])
    chg[me] = jnp.sum(moved.reshape(piece // 8, 8, LANES), axis=0)

    def e_copy(i, slot):
        return remote(chg.at[me], chg.at[slot], e_s.at[i], e_r.at[slot], i // n_col, i % n_col)

    others(n_row * n_col, me, lambda i: e_copy(i, me).start())
    rank_ref[...] = last
    others(n_row, r, lambda i: deg_copy(i, r).wait_send())
    others(n_col, c, lambda i: lost_copy(lost1, l1_s, l1_r, i, c).wait_send())
    others(n_col, c, lambda i: lost_copy(lost2, l2_s, l2_r, i, c).wait_send())

    def b_sent(q):
        @pl.when(jnp.logical_not(jnp.logical_and(diagonal, q == r)))
        def _():
            b_copy(q, c).wait_send()

    each(n_row, b_sent)
    others(n_row, r, lambda i: c_copy(i, r).wait_send())

    @pl.when(jnp.logical_not(diagonal))
    def _():
        t_copy.wait_send()

    others(n_col, c, lambda i: d_copy(i, c).wait_send())
    others(n_row * n_col, me, lambda i: e_copy(i, i).wait_recv())
    total = lax.fori_loop(0, n_row * n_col, lambda i, x: x + chg[i],
                          jnp.zeros((8, LANES), jnp.float32))
    change_ref[...] = jnp.sum(total, axis=0, keepdims=True) / host_total
    others(n_row * n_col, me, lambda i: e_copy(i, me).wait_send())


def shards(n_row, n_col, tile_bits, tile_rows, tile_cols, tile_count, host_order, seed_hosts,
           dangling):
    packed = tile_bits[0, 0]
    slots, words, block = packed.shape
    host_total = host_order.shape[0]
    range_hosts = dangling.shape[0]
    blocks = range_hosts // block
    topics, seeds = seed_hosts.shape
    piece = range_hosts // n_col
    assert slots < 128 and topics == LANES and n_row == n_col and piece % block == 0
    seed_scale = host_total / (16.0 * seeds)
    f32, bf16, i32 = jnp.float32, jnp.bfloat16, jnp.int32
    chunks = range_hosts // LANES
    high_rows = -(-(range_hosts + piece) // (LANES * 8)) * 8
    vmem = pl.BlockSpec(memory_space=pltpu.VMEM)
    smem = pl.BlockSpec(memory_space=pltpu.SMEM)
    adjacency, degree, tele_src, tele_own = pl.pallas_call(
        functools.partial(cell_kernel, (range_hosts, piece, block, blocks, seed_scale)),
        out_shape=[
            jax.ShapeDtypeStruct((range_hosts, range_hosts), bf16),
            jax.ShapeDtypeStruct((chunks, LANES), f32),
            jax.ShapeDtypeStruct((range_hosts, topics), f32),
            jax.ShapeDtypeStruct((piece, topics), f32),
        ],
        in_specs=[smem, smem, smem, pl.BlockSpec(memory_space=pl.ANY), vmem, vmem],
        out_specs=[vmem] * 4,
        scratch_shapes=[
            pltpu.VMEM((slots, words, block), i32),
            pltpu.VMEM((blocks * blocks, 2, words, block), i32),
            pltpu.VMEM((blocks, words, block), i32),
            pltpu.VMEM((topics, seeds), i32),
            pltpu.VMEM((topics * high_rows, LANES), f32),
            pltpu.SemaphoreType.DMA,
        ],
        compiler_params=pltpu.CompilerParams(vmem_limit_bytes=60 * 2**20),
        name="cell",
    )(tile_rows[0, 0], tile_cols[0, 0], tile_count[0], packed,
      host_order.reshape(host_total // LANES, LANES), seed_hosts)

    devices = n_row * n_col
    dma = lambda n: pltpu.SemaphoreType.DMA((n,))
    rank, change = pl.pallas_call(
        functools.partial(rank_kernel, (n_row, n_col, range_hosts, piece, block, host_total)),
        out_shape=[
            jax.ShapeDtypeStruct((piece, topics), f32),
            jax.ShapeDtypeStruct((1, topics), f32),
        ],
        in_specs=[vmem] * 5,
        out_specs=[vmem] * 2,
        scratch_shapes=[
            pltpu.VMEM((n_row, chunks, LANES), f32),
            pltpu.VMEM((chunks, LANES), f32),
            pltpu.VMEM((chunks, LANES), f32),
            pltpu.VMEM((range_hosts, topics), f32),
            pltpu.VMEM((range_hosts, topics), f32),
            pltpu.VMEM((range_hosts, topics), bf16),
            pltpu.VMEM((piece, topics), f32),
            pltpu.VMEM((piece, topics), f32),
            pltpu.VMEM((n_row, piece, topics), bf16),
            pltpu.VMEM((n_col, piece, topics), bf16),
            pltpu.VMEM((n_col, piece, topics), bf16),
            pltpu.VMEM((n_row, piece, topics), bf16),
            pltpu.VMEM((piece, topics), f32),
            pltpu.VMEM((piece, topics), f32),
            pltpu.VMEM((n_col, piece, topics), bf16),
            pltpu.VMEM((n_col, 8, topics), f32),
            pltpu.VMEM((n_col, 8, topics), f32),
            pltpu.VMEM((devices, 8, topics), f32),
            dma(n_row), dma(n_row),
            dma(n_col), dma(n_col), dma(n_col), dma(n_col),
            dma(n_row), dma(n_col),
            dma(n_row), dma(n_row),
            pltpu.SemaphoreType.DMA, pltpu.SemaphoreType.DMA,
            dma(n_col), dma(n_col),
            dma(devices), dma(devices),
        ],
        compiler_params=pltpu.CompilerParams(
            collective_id=0, has_side_effects=True, vmem_limit_bytes=60 * 2**20),
        name="iterate",
    )(adjacency, degree, dangling.reshape(chunks, LANES), tele_src, tele_own)
    return (rank, change.reshape(topics))


def solution(mesh):
    in_specs = (
        P(("groups", "row"), "col", None, None, None),
        P(("groups", "row"), "col", None),
        P(("groups", "row"), "col", None),
        P(("groups", "row"), "col"),
        P("groups"),
        P("groups", None),
        P(("groups", "col")),
    )
    out_specs = (P(("groups", "row", "col"), None), P("groups"))
    body = functools.partial(shards, mesh.shape["row"], mesh.shape["col"])
    return jax.shard_map(body, mesh=mesh, in_specs=in_specs, out_specs=out_specs, check_vma=False)
```

time: 848 us -> 62.5 us (0.07)
  other arithmetic: 379 us -> 0 us
  local copies, waits for them, and re-layouts: 225 us -> 2.69 us
  blocking collectives: 114 us -> 0 us
  matrix products: 59.3 us -> 0 us
  Pallas kernels: 0 us -> 58.6 us
  waiting for transfers between devices: 51.8 us -> 0 us
  between operations: 14.7 us -> 1.29 us
    unnamed x7 -> x0, other arithmetic: 343 us -> none
    gather x1 -> x0, local copies, waits for them, and re-layouts: 181 us -> none  [shards(): positions = host_order[seed_hosts]]
    psum x4 -> x0, blocking collectives: 100 us -> none  [the longest x2 60.2 us: lost_total(): lax.psum(jnp.sum(rank_own, axis=0) - jnp.sum(flow_own, axis=0), ('row', '...]
    dot_general x84 -> x0, matrix products: 59.3 us -> none  [the longest x24 34.2 us: add_group(): jnp.einsum('gb,gik->bik', placing, product, precision=lax.Precision.HIGHEST)]
    pallas_call x0 -> x2, Pallas kernels: none -> 58.6 us  [the longest x1 44.9 us: shards(): pl.pallas_call(functools.partial(rank_kernel, (n_row, n_col, range_hosts,...]
    dynamic_slice x96 -> x0, local copies, waits for them, and re-layouts: 39.8 us -> none  [the longest x36 35 us: group_tiles(): packed_words = lax.dynamic_slice_in_dim(packed, first_slot, slot_group, 0)]
    psum x1 -> x0, waiting for transfers between devices: 31.3 us -> none  [from_root(): return lax.psum(block, axis)]
    convert_element_type x39 -> x0, other arithmetic: 24.8 us -> none  [the longest x36 23.5 us: group_tiles(): live_slots.astype(jnp.int32)[:, None, None]]
  transfers between devices with their start and end apart: 3 -> 0, of which waited for: 2 -> 0; matrix products, arithmetic and copies ran while one was open for 20% -> 0% of each run, Pallas kernels for 0% -> 0%
where the time goes in v1:
time: 62.5 us
  Pallas kernels  58.6 us (94%)
  local copies, waits for them, and re-layouts  2.69 us (4%)
  between operations  1.29 us (2%)
    pallas_call x1, Pallas kernels, shards(): pl.pallas_call(functools.partial(rank_kernel, (n_row, n_col, range_hosts,...  44.9 us
    pallas_call x1, Pallas kernels, shards(): pl.pallas_call(functools.partial(cell_kernel, (range_hosts, piece, block,...  13.7 us
    unnamed x2, local copies, waits for them, and re-layouts  2.69 us

profile of v1, /device:TPU:0, one launch (start us, length us, event | category | flops | bytes accessed | tf_op | source)
XLA Modules:
  0.0 62.5 jit_solution(16283588367927134334)
XLA Ops:
  1.3 13.7 %cell.1 = (bf16[1024,1024]{1,0:T(8,128)(2,1)}, f32[8,128]{1,0:T(8,128)}, f32[1024,128]{1,0:T(8,128)}, f32[256,128]{1,0:T(8,128)}) custom-call(s32[96]{0:T(128)} %bitcast.11, s32[96]{0:T(128)} %bitcast.12, s32[1]{0:T(128)} %bitcast.7.count_ref, s32[96,32,256]{2,1,0:T(8,128)} %bitcast.8, s32[32,128]{1,0:T(8,128)} %bitcast.9, s32[128,256]{1,0:T(8,128)} %seeds_ref.1), custom_call_target="tpu_custom_call" | custom-call | tf_op jit(solution)/shard_map/cell/pallas_call | solution.py:338
  14.9 44.9 %iterate.1 = (f32[256,128]{1,0:T(8,128)}, f32[1,128]{1,0:T(1,128)}) custom-call(bf16[1024,1024]{1,0:T(8,128)(2,1)} %get-tuple-element.8.a_ref, f32[8,128]{1,0:T(8,128)} %get-tuple-element.9.deg_ref, s32[8,128]{1,0:T(8,128)} %bitcast.10, f32[1024,128]{1,0:T(8,128)} %get-tuple-element.10.src_ref, f32[256,128]{1,0:T(8,128)} %get-tuple-element.11.own_ref), custom_call_target="tpu_custom_call" | custom-call | tf_op jit(solution)/shard_map/iterate/pallas_call | solution.py:363
  59.8 1.6 %copy.12 = f32[256,128]{1,0:T(8,128)} copy(f32[256,128]{1,0:T(8,128)} %get-tuple-element.16) | data formatting | bytes 262144
  61.4 1.1 %copy.13 = f32[128]{0:T(128)} copy(f32[128]{0:T(128)} %bitcast.13) | data formatting | bytes 1024

commit v2 on v1

--- a/solution.py
+++ b/solution.py
@@ -12,71 +12,14 @@
 
 
 def cell_kernel(
-    sizes, rows_ref, cols_ref, count_ref, bits_hbm, order_ref, seeds_ref,
-    a_ref, deg_ref, src_ref, own_ref, bits, acc, dacc, pos, hist, sem,
+    sizes, rows_ref, cols_ref, count_ref, bits_hbm, a_ref, deg_ref, bits, acc, dacc, sem,
 ):
-    range_hosts, piece, block, blocks, seed_scale = sizes
+    block, blocks = sizes
     words = block // 8
-    topics, seeds = seeds_ref.shape
-    row_index = lax.axis_index("row")
-    col_index = lax.axis_index("col")
     fetch = pltpu.make_async_copy(bits_hbm, bits, sem)
     fetch.start()
     acc[...] = jnp.zeros_like(acc)
     dacc[...] = jnp.zeros_like(dacc)
-
-    table_rows = order_ref.shape[0]
-    parts = seeds // LANES
-
-    def place(group, carry):
-        rows8 = pl.ds(pl.multiple_of(group * 8, 8), 8)
-        ids = [seeds_ref[rows8, h * LANES:(h + 1) * LANES] for h in range(parts)]
-        low = [x & (LANES - 1) for x in ids]
-        high = [x >> 7 for x in ids]
-
-        def look(t, found):
-            row = jnp.broadcast_to(order_ref[pl.ds(t, 1), :], (8, LANES))
-            return tuple(
-                jnp.where(high[h] == t,
-                          jnp.take_along_axis(row, low[h], axis=1, mode="promise_in_bounds"),
-                          found[h])
-                for h in range(parts)
-            )
-
-        found = lax.fori_loop(0, table_rows, look,
-                              tuple(jnp.zeros((8, LANES), jnp.int32) for _ in range(parts)),
-                              unroll=8)
-        for h in range(parts):
-            pos[rows8, h * LANES:(h + 1) * LANES] = found[h]
-        return carry
-
-    lax.fori_loop(0, topics // 8, place, 0)
-
-    src_high = range_hosts // LANES
-    own_high = piece // LANES
-    high_rows = hist.shape[0] // topics
-    t = lax.broadcasted_iota(jnp.int32, (high_rows, seeds), 0)
-    first_src = col_index * src_high
-    first_own = row_index * src_high + col_index * own_high
-    wanted = jnp.where(t < src_high, first_src + t,
-                       jnp.where(t < src_high + own_high, first_own + t - src_high, -1))
-    lane_id = lax.broadcasted_iota(jnp.int32, (LANES, seeds), 0)
-
-    def count(k, carry):
-        row = pos[pl.ds(k, 1), :]
-        low = jnp.where((row & (LANES - 1)) == lane_id, 1.0, 0.0).astype(jnp.bfloat16)
-        high = jnp.where((row >> 7) == wanted, 1.0, 0.0).astype(jnp.bfloat16)
-        hist[pl.ds(pl.multiple_of(k * high_rows, 8), high_rows), :] = lax.dot_general(
-            high, low, (((1,), (1,)), ((), ())), preferred_element_type=jnp.float32)
-        return carry
-
-    lax.fori_loop(0, topics, count, 0, unroll=8)
-    for i in range(src_high):
-        src_ref[i * LANES:(i + 1) * LANES, :] = (
-            hist[pl.ds(i, topics, stride=high_rows), :].T * seed_scale)
-    for i in range(own_high):
-        own_ref[i * LANES:(i + 1) * LANES, :] = (
-            hist[pl.ds(src_high + i, topics, stride=high_rows), :].T * seed_scale)
 
     fetch.wait()
 
@@ -115,12 +58,14 @@
 
 
 def rank_kernel(
-    sizes, a_ref, deg_ref, dang_ref, src_ref, own_ref, rank_ref, change_ref,
-    degs, wrow, drow, wcol, dcol, scaled, nat, own_flow, sbuf1, sbuf2, recv_b, recv_c, recv_t,
-    rank1, recv_d, lost1, lost2, chg,
-    deg_s, deg_r, l1_s, l1_r, l2_s, l2_r, b_s, b_r, c_s, c_r, t_s, t_r, d_s, d_r, e_s, e_r,
+    sizes, a_hbm, deg_ref, dang_ref, order_ref, seeds_ref, rank_ref, change_ref,
+    a_ref, pos, hist, hist_bf, src_ref, tele_bf, own_bf,
+    degs, wcol, dcol, scaled, nat, own_flow, sbuf1, sbuf2, recv_b, recv_c, recv_t,
+    rank1, recv_d, lost1, lost2, chg, a_sem,
+    deg_s, deg_r, h_s, h_r, o_s, o_r, l1_s, l1_r, l2_s, l2_r, b_s, b_r, c_s, c_r, t_s, t_r,
+    d_s, d_r, e_s, e_r,
 ):
-    n_row, n_col, range_hosts, piece, block, host_total = sizes
+    n_row, n_col, range_hosts, piece, block, host_total, seed_scale = sizes
     words = block // 8
     r = lax.axis_index("row")
     c = lax.axis_index("col")
@@ -146,26 +91,91 @@
     barrier = pltpu.get_barrier_semaphore()
     others(n_row * n_col, me, lambda i: pl.semaphore_signal(
         barrier, inc=1, device_id={"row": i // n_col, "col": i % n_col}, device_id_type=MESH))
+
+    fetch = pltpu.make_async_copy(a_hbm, a_ref, a_sem)
+    fetch.start()
+    topics, seeds = seeds_ref.shape
+    share = topics // n_row
+    table_rows = order_ref.shape[0]
+    parts = seeds // LANES
+
+    def place(group, carry):
+        rows8 = pl.ds(pl.multiple_of(r * share + group * 8, 8), 8)
+        ids = [seeds_ref[rows8, h * LANES:(h + 1) * LANES] for h in range(parts)]
+        low = [x & (LANES - 1) for x in ids]
+        high = [x >> 7 for x in ids]
+
+        def look(t, found):
+            row = jnp.broadcast_to(order_ref[pl.ds(t, 1), :], (8, LANES))
+            return tuple(
+                jnp.where(high[h] == t,
+                          jnp.take_along_axis(row, low[h], axis=1, mode="promise_in_bounds"),
+                          found[h])
+                for h in range(parts)
+            )
+
+        found = lax.fori_loop(0, table_rows, look,
+                              tuple(jnp.zeros((8, LANES), jnp.int32) for _ in range(parts)),
+                              unroll=8)
+        for h in range(parts):
+            pos[pl.ds(pl.multiple_of(group * 8, 8), 8), h * LANES:(h + 1) * LANES] = found[h]
+        return carry
+
+    lax.fori_loop(0, share // 8, place, 0)
+    wanted = c * chunks + lax.broadcasted_iota(jnp.int32, (chunks, seeds), 0)
+    lane_id = lax.broadcasted_iota(jnp.int32, (LANES, seeds), 0)
+
+    def count(k, carry):
+        row = pos[pl.ds(k, 1), :]
+        low = jnp.where((row & (LANES - 1)) == lane_id, 1.0, 0.0).astype(jnp.bfloat16)
+        high = jnp.where((row >> 7) == wanted, 1.0, 0.0).astype(jnp.bfloat16)
+        hist[pl.ds(pl.multiple_of(k * chunks, 8), chunks), :] = lax.dot_general(
+            high, low, (((1,), (1,)), ((), ())), preferred_element_type=jnp.float32)
+        return carry
+
+    lax.fori_loop(0, share, count, 0, unroll=8)
+    hist_bf[r] = hist[pl.ds(0, share * chunks), :].astype(jnp.bfloat16)
     pl.semaphore_wait(barrier, n_row * n_col - 1)
 
     def deg_copy(i, slot):
         return remote(deg_ref, degs.at[slot], deg_s.at[i], deg_r.at[slot], i, c)
 
+    def hist_copy(i, slot):
+        return remote(hist_bf.at[r], hist_bf.at[slot], h_s.at[i], h_r.at[slot], i, c)
+
     others(n_row, r, lambda i: deg_copy(i, r).start())
+    others(n_row, r, lambda i: hist_copy(i, r).start())
     degs[r] = deg_ref[...]
     others(n_row, r, lambda i: deg_copy(i, i).wait_recv())
     degree = degs[0]
     for i in range(1, n_row):
         degree = degree + degs[i]
-    wrow[...] = (1.0 - dang_ref[...].astype(jnp.float32)) / jnp.maximum(degree, 1.0)
-    drow[...] = degree
-
-    def spread(i):
-        rows = pl.ds(pl.multiple_of(i * LANES, LANES), LANES)
-        wcol[rows, :] = jnp.broadcast_to(wrow[pl.ds(i, 1), :], (LANES, LANES)).T
-        dcol[rows, :] = jnp.broadcast_to(drow[pl.ds(i, 1), :], (LANES, LANES)).T
-
-    each(chunks, spread)
+    weight = ((1.0 - dang_ref[...].astype(jnp.float32)) / jnp.maximum(degree, 1.0)).T
+    degree = degree.T
+    for i in range(chunks):
+        rows = slice(i * LANES, (i + 1) * LANES)
+        wcol[rows, :] = jnp.broadcast_to(weight[:, i:i + 1], (LANES, LANES))
+        dcol[rows, :] = jnp.broadcast_to(degree[:, i:i + 1], (LANES, LANES))
+
+    others(n_row, r, lambda i: hist_copy(i, i).wait_recv())
+    slab = share * chunks
+    for i in range(n_row):
+        hist[i * slab:(i + 1) * slab, :] = hist_bf[i].astype(jnp.float32)
+    for i in range(chunks):
+        tele_bf[i * LANES:(i + 1) * LANES, :] = (
+            hist[pl.ds(i, topics, stride=chunks), :].T.astype(jnp.bfloat16))
+    src_ref[...] = tele_bf[...].astype(jnp.float32) * seed_scale
+    diagonal = r == c
+    quarter = pl.ds(pl.multiple_of(r * piece, piece), piece)
+    o_copy = remote(tele_bf.at[quarter], own_bf, o_s, o_r, c, r)
+
+    @pl.when(jnp.logical_not(diagonal))
+    def _():
+        o_copy.start()
+
+    @pl.when(diagonal)
+    def _():
+        own_bf[...] = tele_bf[quarter, :]
 
     def make_scaled(source_of, lost, send, recv):
         def step(i, total):
@@ -200,7 +210,7 @@
         sbuf[q] = nat[...].astype(jnp.bfloat16)
 
     make_scaled(lambda i, rows: src_ref[rows, :].astype(jnp.bfloat16), lost1, l1_s, l1_r)
-    diagonal = r == c
+    fetch.wait()
 
     def b_copy(q, slot):
         return remote(sbuf1.at[q], recv_b.at[slot], b_s.at[q], b_r.at[slot], q, r)
@@ -230,7 +240,7 @@
     flow = recv_b[0].astype(jnp.float32)
     for i in range(1, n_col):
         flow = flow + recv_b[i].astype(jnp.float32)
-    tele = src_ref[pl.ds(pl.multiple_of(r * piece, piece), piece), :]
+    tele = src_ref[quarter, :]
     new_rank = 0.85 * flow + share1 * tele
     recv_c[r] = new_rank.astype(jnp.bfloat16)
 
@@ -281,12 +291,13 @@
     @pl.when(jnp.logical_not(diagonal))
     def _():
         t_copy.wait_recv()
+        o_copy.wait_recv()
 
     others(n_col, c, lambda i: d_copy(0, i).wait_recv())
     flow = own_flow[...]
     for i in range(n_col):
         flow = flow + recv_d[i].astype(jnp.float32)
-    last = 0.85 * flow + share2 * own_ref[...]
+    last = 0.85 * flow + share2 * (own_bf[...].astype(jnp.float32) * seed_scale)
     moved = jnp.abs(last - recv_t[...])
     chg[me] = jnp.sum(moved.reshape(piece // 8, 8, LANES), axis=0)
 
@@ -296,6 +307,7 @@
     others(n_row * n_col, me, lambda i: e_copy(i, me).start())
     rank_ref[...] = last
     others(n_row, r, lambda i: deg_copy(i, r).wait_send())
+    others(n_row, r, lambda i: hist_copy(i, r).wait_send())
     others(n_col, c, lambda i: lost_copy(lost1, l1_s, l1_r, i, c).wait_send())
     others(n_col, c, lambda i: lost_copy(lost2, l2_s, l2_r, i, c).wait_send())
 
@@ -310,13 +322,19 @@
     @pl.when(jnp.logical_not(diagonal))
     def _():
         t_copy.wait_send()
+        o_copy.wait_send()
 
     others(n_col, c, lambda i: d_copy(i, c).wait_send())
     others(n_row * n_col, me, lambda i: e_copy(i, i).wait_recv())
     total = lax.fori_loop(0, n_row * n_col, lambda i, x: x + chg[i],
                           jnp.zeros((8, LANES), jnp.float32))
-    change_ref[...] = jnp.sum(total, axis=0, keepdims=True) / host_total
+    change_ref[...] = total
     others(n_row * n_col, me, lambda i: e_copy(i, me).wait_send())
+
+
+def give_kernel(host_total, last_ref, moved_ref, rank_ref, change_ref):
+    rank_ref[...] = last_ref[...]
+    change_ref[...] = jnp.sum(moved_ref[...], axis=0, keepdims=True) / host_total
 
 
 def shards(n_row, n_col, tile_bits, tile_rows, tile_cols, tile_count, host_order, seed_hosts,
@@ -329,49 +347,51 @@
     topics, seeds = seed_hosts.shape
     piece = range_hosts // n_col
     assert slots < 128 and topics == LANES and n_row == n_col and piece % block == 0
+    assert seeds <= 256 and topics % (8 * n_row) == 0
     seed_scale = host_total / (16.0 * seeds)
     f32, bf16, i32 = jnp.float32, jnp.bfloat16, jnp.int32
     chunks = range_hosts // LANES
-    high_rows = -(-(range_hosts + piece) // (LANES * 8)) * 8
     vmem = pl.BlockSpec(memory_space=pltpu.VMEM)
     smem = pl.BlockSpec(memory_space=pltpu.SMEM)
-    adjacency, degree, tele_src, tele_own = pl.pallas_call(
-        functools.partial(cell_kernel, (range_hosts, piece, block, blocks, seed_scale)),
+    hbm = pl.BlockSpec(memory_space=pl.ANY)
+    adjacency, degree = pl.pallas_call(
+        functools.partial(cell_kernel, (block, blocks)),
         out_shape=[
             jax.ShapeDtypeStruct((range_hosts, range_hosts), bf16),
             jax.ShapeDtypeStruct((chunks, LANES), f32),
-            jax.ShapeDtypeStruct((range_hosts, topics), f32),
-            jax.ShapeDtypeStruct((piece, topics), f32),
         ],
-        in_specs=[smem, smem, smem, pl.BlockSpec(memory_space=pl.ANY), vmem, vmem],
-        out_specs=[vmem] * 4,
+        in_specs=[smem, smem, smem, hbm],
+        out_specs=[vmem] * 2,
         scratch_shapes=[
             pltpu.VMEM((slots, words, block), i32),
             pltpu.VMEM((blocks * blocks, 2, words, block), i32),
             pltpu.VMEM((blocks, words, block), i32),
-            pltpu.VMEM((topics, seeds), i32),
-            pltpu.VMEM((topics * high_rows, LANES), f32),
             pltpu.SemaphoreType.DMA,
         ],
         compiler_params=pltpu.CompilerParams(vmem_limit_bytes=60 * 2**20),
         name="cell",
-    )(tile_rows[0, 0], tile_cols[0, 0], tile_count[0], packed,
-      host_order.reshape(host_total // LANES, LANES), seed_hosts)
+    )(tile_rows[0, 0], tile_cols[0, 0], tile_count[0], packed)
 
     devices = n_row * n_col
     dma = lambda n: pltpu.SemaphoreType.DMA((n,))
-    rank, change = pl.pallas_call(
-        functools.partial(rank_kernel, (n_row, n_col, range_hosts, piece, block, host_total)),
+    last, moved = pl.pallas_call(
+        functools.partial(rank_kernel, (n_row, n_col, range_hosts, piece, block, host_total,
+                                        seed_scale)),
         out_shape=[
             jax.ShapeDtypeStruct((piece, topics), f32),
-            jax.ShapeDtypeStruct((1, topics), f32),
+            jax.ShapeDtypeStruct((8, topics), f32),
         ],
-        in_specs=[vmem] * 5,
+        in_specs=[hbm] + [vmem] * 4,
         out_specs=[vmem] * 2,
         scratch_shapes=[
+            pltpu.VMEM((range_hosts, range_hosts), bf16),
+            pltpu.VMEM((topics // n_row, seeds), i32),
+            pltpu.VMEM((topics * chunks, LANES), f32),
+            pltpu.VMEM((n_row, topics // n_row * chunks, LANES), bf16),
+            pltpu.VMEM((range_hosts, topics), f32),
+            pltpu.VMEM((range_hosts, topics), bf16),
+            pltpu.VMEM((piece, topics), bf16),
             pltpu.VMEM((n_row, chunks, LANES), f32),
-            pltpu.VMEM((chunks, LANES), f32),
-            pltpu.VMEM((chunks, LANES), f32),
             pltpu.VMEM((range_hosts, topics), f32),
             pltpu.VMEM((range_hosts, topics), f32),
             pltpu.VMEM((range_hosts, topics), bf16),
@@ -387,7 +407,9 @@
             pltpu.VMEM((n_col, 8, topics), f32),
             pltpu.VMEM((n_col, 8, topics), f32),
             pltpu.VMEM((devices, 8, topics), f32),
-            dma(n_row), dma(n_row),
+            pltpu.SemaphoreType.DMA,
+            dma(n_row), dma(n_row), dma(n_row), dma(n_row),
+            pltpu.SemaphoreType.DMA, pltpu.SemaphoreType.DMA,
             dma(n_col), dma(n_col), dma(n_col), dma(n_col),
             dma(n_row), dma(n_col),
             dma(n_row), dma(n_row),
@@ -398,7 +420,18 @@
         compiler_params=pltpu.CompilerParams(
             collective_id=0, has_side_effects=True, vmem_limit_bytes=60 * 2**20),
         name="iterate",
-    )(adjacency, degree, dangling.reshape(chunks, LANES), tele_src, tele_own)
+    )(adjacency, degree, dangling.reshape(chunks, LANES),
+      host_order.reshape(host_total // LANES, LANES), seed_hosts)
+    rank, change = pl.pallas_call(
+        functools.partial(give_kernel, host_total),
+        out_shape=[
+            jax.ShapeDtypeStruct((piece, topics), f32),
+            jax.ShapeDtypeStruct((1, topics), f32),
+        ],
+        in_specs=[vmem] * 2,
+        out_specs=[vmem] * 2,
+        name="give",
+    )(last, moved)
     return (rank, change.reshape(topics))
 
 

time: 62.5 us -> 56.8 us (0.909)
  Pallas kernels: 58.6 us -> 55 us
  local copies, waits for them, and re-layouts: 2.69 us -> 0 us
    pallas_call x1 -> x2, Pallas kernels: 13.7 us -> 6.38 us  [the longest x1 4.8 us: shards(): pl.pallas_call(functools.partial(cell_kernel, (block, blocks)), out_shape...]
    pallas_call x1, Pallas kernels: 44.9 us -> 48.6 us  [shards(): pl.pallas_call(functools.partial(rank_kernel, (n_row, n_col, range_hosts,...]
    unnamed x2 -> x0, local copies, waits for them, and re-layouts: 2.69 us -> none
where the time goes in v2:
time: 56.8 us; the launch traced here: 56.3 us
  Pallas kernels  55 us (97%)
  between operations  1.29 us (2%)
    pallas_call x1, Pallas kernels, shards(): pl.pallas_call(functools.partial(rank_kernel, (n_row, n_col, range_hosts,...  48.6 us
    pallas_call x1, Pallas kernels, shards(): pl.pallas_call(functools.partial(cell_kernel, (block, blocks)), out_shape...  4.8 us
    pallas_call x1, Pallas kernels, shards(): pl.pallas_call(functools.partial(give_kernel, host_total), out_shape=[jax...  1.57 us

profile of v2, /device:TPU:0, one launch (start us, length us, event | category | flops | bytes accessed | tf_op | source)
XLA Modules:
  0.0 56.3 jit_solution(15659889706763605930)
XLA Ops:
  1.3 4.8 %cell.1 = (bf16[1024,1024]{1,0:T(8,128)(2,1)}, f32[8,128]{1,0:T(8,128)}) custom-call(s32[96]{0:T(128)} %bitcast.11, s32[96]{0:T(128)} %bitcast.12, s32[1]{0:T(128)} %bitcast.7.count_ref, s32[96,32,256]{2,1,0:T(8,128)} %bitcast.8), custom_call_target="tpu_custom_call" | custom-call | tf_op jit(solution)/shard_map/cell/pallas_call | solution.py:357
  6.1 48.6 %iterate.1 = (f32[256,128]{1,0:T(8,128)}, f32[8,128]{1,0:T(8,128)}) custom-call(bf16[1024,1024]{1,0:T(8,128)(2,1)} %get-tuple-element.8.a_hbm, f32[8,128]{1,0:T(8,128)} %get-tuple-element.9.deg_ref, s32[8,128]{1,0:T(8,128)} %bitcast.10, s32[32,128]{1,0:T(8,128)} %bitcast.9, s32[128,256]{1,0:T(8,128)} %seeds_ref.1), custom_call_target="tpu_custom_call" | custom-call | tf_op jit(solution)/shard_map/iterate/pallas_call | solution.py:377
  54.7 1.6 %give.1 = (f32[256,128]{1,0:T(8,128)}, f32[1,128]{1,0:T(1,128)}) custom-call(f32[256,128]{1,0:T(8,128)} %get-tuple-element.10.last_ref, f32[8,128]{1,0:T(8,128)} %get-tuple-element.11.moved_ref), custom_call_target="tpu_custom_call" | custom-call | tf_op jit(solution)/shard_map/give/pallas_call | solution.py:425

commit v3 on v2

--- a/solution.py
+++ b/solution.py
@@ -61,15 +61,14 @@
     sizes, a_hbm, deg_ref, dang_ref, order_ref, seeds_ref, rank_ref, change_ref,
     a_ref, pos, hist, hist_bf, src_ref, tele_bf, own_bf,
     degs, wcol, dcol, scaled, nat, own_flow, sbuf1, sbuf2, recv_b, recv_c, recv_t,
-    rank1, recv_d, lost1, lost2, chg, a_sem,
+    rank1, recv_d, lost1, lost2, chg, chg_all, stage, a_sem,
     deg_s, deg_r, h_s, h_r, o_s, o_r, l1_s, l1_r, l2_s, l2_r, b_s, b_r, c_s, c_r, t_s, t_r,
-    d_s, d_r, e_s, e_r,
+    d_s, d_r, e_s, e_r, f_s, f_r, s_s, s_r,
 ):
     n_row, n_col, range_hosts, piece, block, host_total, seed_scale = sizes
     words = block // 8
     r = lax.axis_index("row")
     c = lax.axis_index("col")
-    me = r * n_col + c
     total_mass = host_total / 16.0
     chunks = range_hosts // LANES
 
@@ -89,8 +88,19 @@
             device_id={"row": row, "col": col}, device_id_type=MESH)
 
     barrier = pltpu.get_barrier_semaphore()
-    others(n_row * n_col, me, lambda i: pl.semaphore_signal(
-        barrier, inc=1, device_id={"row": i // n_col, "col": i % n_col}, device_id_type=MESH))
+    diagonal = r == c
+
+    def greet(row, col):
+        pl.semaphore_signal(barrier, inc=1, device_id={"row": row, "col": col},
+                            device_id_type=MESH)
+
+    others(n_row, r, lambda i: greet(i, c))
+    others(n_col, c, lambda i: greet(r, i))
+
+    @pl.when(jnp.logical_not(diagonal))
+    def _():
+        greet(c, r)
+
 
     fetch = pltpu.make_async_copy(a_hbm, a_ref, a_sem)
     fetch.start()
@@ -135,7 +145,7 @@
 
     lax.fori_loop(0, share, count, 0, unroll=8)
     hist_bf[r] = hist[pl.ds(0, share * chunks), :].astype(jnp.bfloat16)
-    pl.semaphore_wait(barrier, n_row * n_col - 1)
+    pl.semaphore_wait(barrier, n_row + n_col - 2 + jnp.where(diagonal, 0, 1))
 
     def deg_copy(i, slot):
         return remote(deg_ref, degs.at[slot], deg_s.at[i], deg_r.at[slot], i, c)
@@ -165,17 +175,8 @@
         tele_bf[i * LANES:(i + 1) * LANES, :] = (
             hist[pl.ds(i, topics, stride=chunks), :].T.astype(jnp.bfloat16))
     src_ref[...] = tele_bf[...].astype(jnp.float32) * seed_scale
-    diagonal = r == c
     quarter = pl.ds(pl.multiple_of(r * piece, piece), piece)
     o_copy = remote(tele_bf.at[quarter], own_bf, o_s, o_r, c, r)
-
-    @pl.when(jnp.logical_not(diagonal))
-    def _():
-        o_copy.start()
-
-    @pl.when(diagonal)
-    def _():
-        own_bf[...] = tele_bf[quarter, :]
 
     def make_scaled(source_of, lost, send, recv):
         def step(i, total):
@@ -212,31 +213,42 @@
     make_scaled(lambda i, rows: src_ref[rows, :].astype(jnp.bfloat16), lost1, l1_s, l1_r)
     fetch.wait()
 
-    def b_copy(q, slot):
-        return remote(sbuf1.at[q], recv_b.at[slot], b_s.at[q], b_r.at[slot], q, r)
+    def s_copy(q, slot):
+        return remote(sbuf1.at[q], stage.at[slot], s_s.at[q], s_r.at[slot], q, c)
+
+    def b_copy(i, slot):
+        return remote(stage.at[i], recv_b.at[slot], b_s.at[i], b_r.at[slot], r, i)
 
     def first_piece(i):
         q = lax.rem(r + 1 + i, n_row)
         flow_piece(q, sbuf1)
-        home = jnp.logical_and(diagonal, q == r)
-
-        @pl.when(jnp.logical_not(home))
-        def _():
-            b_copy(q, c).start()
-
-        @pl.when(home)
-        def _():
-            recv_b[c] = sbuf1[q]
+
+        @pl.when(q != r)
+        def _():
+            s_copy(q, r).start()
+
+        @pl.when(q == r)
+        def _():
+            stage[r] = sbuf1[q]
 
     each(n_row, first_piece)
+
+    def pass_on(j):
+        i = lax.rem(r + n_row - j, n_row)
+
+        @pl.when(i != r)
+        def _():
+            s_copy(0, i).wait_recv()
+
+        @pl.when(i != c)
+        def _():
+            b_copy(i, c).start()
+
+    each(n_row, pass_on)
+    recv_b[c] = stage[c]
     share1 = coefficient(lost1, l1_s, l1_r)
 
-    def b_wait(i):
-        @pl.when(jnp.logical_not(jnp.logical_and(diagonal, i == c)))
-        def _():
-            b_copy(0, i).wait_recv()
-
-    each(n_col, b_wait)
+    others(n_col, c, lambda i: b_copy(0, i).wait_recv())
     flow = recv_b[0].astype(jnp.float32)
     for i in range(1, n_col):
         flow = flow + recv_b[i].astype(jnp.float32)
@@ -254,10 +266,12 @@
     @pl.when(jnp.logical_not(diagonal))
     def _():
         t_copy.start()
+        o_copy.start()
 
     @pl.when(diagonal)
     def _():
         recv_t[...] = rank1[...]
+        own_bf[...] = tele_bf[quarter, :]
 
     others(n_row, r, lambda i: c_copy(i, i).wait_recv())
 
@@ -299,24 +313,29 @@
         flow = flow + recv_d[i].astype(jnp.float32)
     last = 0.85 * flow + share2 * (own_bf[...].astype(jnp.float32) * seed_scale)
     moved = jnp.abs(last - recv_t[...])
-    chg[me] = jnp.sum(moved.reshape(piece // 8, 8, LANES), axis=0)
+    chg[c] = jnp.sum(moved.reshape(piece // 8, 8, LANES), axis=0)
 
     def e_copy(i, slot):
-        return remote(chg.at[me], chg.at[slot], e_s.at[i], e_r.at[slot], i // n_col, i % n_col)
-
-    others(n_row * n_col, me, lambda i: e_copy(i, me).start())
+        return remote(chg.at[c], chg.at[slot], e_s.at[i], e_r.at[slot], r, i)
+
+    def f_copy(i, slot):
+        return remote(chg_all.at[r], chg_all.at[slot], f_s.at[i], f_r.at[slot], i, c)
+
+    others(n_col, c, lambda i: e_copy(i, c).start())
     rank_ref[...] = last
+    others(n_col, c, lambda i: e_copy(i, i).wait_recv())
+    total = chg[0]
+    for i in range(1, n_col):
+        total = total + chg[i]
+    chg_all[r] = total
+    others(n_row, r, lambda i: f_copy(i, r).start())
     others(n_row, r, lambda i: deg_copy(i, r).wait_send())
     others(n_row, r, lambda i: hist_copy(i, r).wait_send())
     others(n_col, c, lambda i: lost_copy(lost1, l1_s, l1_r, i, c).wait_send())
     others(n_col, c, lambda i: lost_copy(lost2, l2_s, l2_r, i, c).wait_send())
 
-    def b_sent(q):
-        @pl.when(jnp.logical_not(jnp.logical_and(diagonal, q == r)))
-        def _():
-            b_copy(q, c).wait_send()
-
-    each(n_row, b_sent)
+    others(n_row, r, lambda i: s_copy(i, r).wait_send())
+    others(n_col, c, lambda i: b_copy(i, c).wait_send())
     others(n_row, r, lambda i: c_copy(i, r).wait_send())
 
     @pl.when(jnp.logical_not(diagonal))
@@ -325,11 +344,13 @@
         o_copy.wait_send()
 
     others(n_col, c, lambda i: d_copy(i, c).wait_send())
-    others(n_row * n_col, me, lambda i: e_copy(i, i).wait_recv())
-    total = lax.fori_loop(0, n_row * n_col, lambda i, x: x + chg[i],
-                          jnp.zeros((8, LANES), jnp.float32))
+    others(n_col, c, lambda i: e_copy(i, c).wait_send())
+    others(n_row, r, lambda i: f_copy(i, i).wait_recv())
+    total = chg_all[0]
+    for i in range(1, n_row):
+        total = total + chg_all[i]
     change_ref[...] = total
-    others(n_row * n_col, me, lambda i: e_copy(i, me).wait_send())
+    others(n_row, r, lambda i: f_copy(i, r).wait_send())
 
 
 def give_kernel(host_total, last_ref, moved_ref, rank_ref, change_ref):
@@ -372,7 +393,6 @@
         name="cell",
     )(tile_rows[0, 0], tile_cols[0, 0], tile_count[0], packed)
 
-    devices = n_row * n_col
     dma = lambda n: pltpu.SemaphoreType.DMA((n,))
     last, moved = pl.pallas_call(
         functools.partial(rank_kernel, (n_row, n_col, range_hosts, piece, block, host_total,
@@ -406,7 +426,9 @@
             pltpu.VMEM((n_col, piece, topics), bf16),
             pltpu.VMEM((n_col, 8, topics), f32),
             pltpu.VMEM((n_col, 8, topics), f32),
-            pltpu.VMEM((devices, 8, topics), f32),
+            pltpu.VMEM((n_col, 8, topics), f32),
+            pltpu.VMEM((n_row, 8, topics), f32),
+            pltpu.VMEM((n_row, piece, topics), bf16),
             pltpu.SemaphoreType.DMA,
             dma(n_row), dma(n_row), dma(n_row), dma(n_row),
             pltpu.SemaphoreType.DMA, pltpu.SemaphoreType.DMA,
@@ -415,7 +437,7 @@
             dma(n_row), dma(n_row),
             pltpu.SemaphoreType.DMA, pltpu.SemaphoreType.DMA,
             dma(n_col), dma(n_col),
-            dma(devices), dma(devices),
+            dma(n_col), dma(n_col), dma(n_row), dma(n_row), dma(n_row), dma(n_row),
         ],
         compiler_params=pltpu.CompilerParams(
             collective_id=0, has_side_effects=True, vmem_limit_bytes=60 * 2**20),

time: 56.8 us -> 52.3 us (0.921)
  Pallas kernels: 55 us -> 50.9 us
    pallas_call x1, Pallas kernels: 48.6 us -> 43.4 us  [shards(): pl.pallas_call(functools.partial(rank_kernel, (n_row, n_col, range_hosts,...]
    pallas_call x1, Pallas kernels: 4.8 us -> 6 us  [shards(): pl.pallas_call(functools.partial(cell_kernel, (block, blocks)), out_shape...]
where the time goes in v3:
time: 52.3 us; the launch traced here: 52.2 us
  Pallas kernels  50.9 us (97%)
  between operations  1.29 us (2%)
    pallas_call x1, Pallas kernels, shards(): pl.pallas_call(functools.partial(rank_kernel, (n_row, n_col, range_hosts,...  43.4 us
    pallas_call x1, Pallas kernels, shards(): pl.pallas_call(functools.partial(cell_kernel, (block, blocks)), out_shape...  6 us
    pallas_call x1, Pallas kernels, shards(): pl.pallas_call(functools.partial(give_kernel, host_total), out_shape=[jax...  1.57 us

profile of v3, /device:TPU:0, one launch (start us, length us, event | category | flops | bytes accessed | tf_op | source)
XLA Modules:
  0.0 52.2 jit_solution(3789367084872596292)
XLA Ops:
  1.3 6.0 %cell.1 = (bf16[1024,1024]{1,0:T(8,128)(2,1)}, f32[8,128]{1,0:T(8,128)}) custom-call(s32[96]{0:T(128)} %bitcast.11, s32[96]{0:T(128)} %bitcast.12, s32[1]{0:T(128)} %bitcast.7.count_ref, s32[96,32,256]{2,1,0:T(8,128)} %bitcast.8), custom_call_target="tpu_custom_call" | custom-call | tf_op jit(solution)/shard_map/cell/pallas_call | solution.py:378
  7.3 43.4 %iterate.1 = (f32[256,128]{1,0:T(8,128)}, f32[8,128]{1,0:T(8,128)}) custom-call(bf16[1024,1024]{1,0:T(8,128)(2,1)} %get-tuple-element.8.a_hbm, f32[8,128]{1,0:T(8,128)} %get-tuple-element.9.deg_ref, s32[8,128]{1,0:T(8,128)} %bitcast.10, s32[32,128]{1,0:T(8,128)} %bitcast.9, s32[128,256]{1,0:T(8,128)} %seeds_ref.1), custom_call_target="tpu_custom_call" | custom-call | tf_op jit(solution)/shard_map/iterate/pallas_call | solution.py:397
  50.7 1.6 %give.1 = (f32[256,128]{1,0:T(8,128)}, f32[1,128]{1,0:T(1,128)}) custom-call(f32[256,128]{1,0:T(8,128)} %get-tuple-element.10.last_ref, f32[8,128]{1,0:T(8,128)} %get-tuple-element.11.moved_ref), custom_call_target="tpu_custom_call" | custom-call | tf_op jit(solution)/shard_map/give/pallas_call | solution.py:447
